TPU v7x, 128 devices: a whole 4x4x4 slice. The times are simulated.
128 devices in a mesh: prompt: 8 (over y_lo, z), resp: 16 (over y_hi, x, core).
Axes of the slice: x: 4, y: 4 (y_hi: 2, y_lo: 2; y = y_hi * 2 + y_lo), z: 4, core: 2. Of those that a mesh axis runs over, the one named last changes fastest.
Arguments:
- queries: bfloat16 [8, 32, 64, 2048], P('prompt', 'resp'), may hold values from -160 to 160
- response_keys: bfloat16 [8, 32, 64, 256], P('prompt', 'resp'), may hold values from -6 to 6
- response_values: bfloat16 [8, 32, 64, 256], P('prompt', 'resp'), may hold values from -6 to 6
- prefix_keys: bfloat16 [8, 512, 256], P('prompt', 'resp'), may hold values from -6 to 6
- prompt_values: bfloat16 [8, 512, 256], P('prompt', 'resp'), may hold values from -6 to 6
- resid: bfloat16 [8, 32, 64, 2048], P('prompt', 'resp'), may hold values from -6 to 6
- out_proj: bfloat16 [2048, 2048], P('prompt'), may hold values from -0.125 to 0.125
- router: bfloat16 [2048, 128], replicated, may hold values from -0.125 to 0.125
- norm_gain: float32 [2048], replicated, may hold values from 0.1 to 1.9
- w_gate: bfloat16 [128, 2048, 768], P(('prompt', 'resp')), may hold values from -0.125 to 0.125
- w_up: bfloat16 [128, 2048, 768], P(('prompt', 'resp')), may hold values from -0.125 to 0.125
- w_down: bfloat16 [128, 768, 2048], P(('prompt', 'resp')), may hold values from -0.21875 to 0.21875
- expert_ids: int32 [8, 32, 64, 4], P('prompt', 'resp'), may hold values from 0 to 127, all different within a row; in each aligned block of 128 rows (0 to 127, 128 to 255, ..., all dimensions but the last counted through in order) at most 6 rows name the same one
- lengths: int32 [8, 32], P('prompt', 'resp'), may hold values from 16 to 64, as said below
- out_grad: bfloat16 [8, 32, 64, 2048], P('prompt', 'resp'), may hold values from -6 to 6
Outputs:
- layer_out: bfloat16 [8, 32, 64, 2048], P('prompt', 'resp')
- resid_grad: bfloat16 [8, 32, 64, 2048], P('prompt', 'resp')
- query_grad: bfloat16 [8, 32, 64, 2048], P('prompt', 'resp')
- resp_key_grad: bfloat16 [8, 32, 64, 256], P('prompt', 'resp')
- resp_value_grad: bfloat16 [8, 32, 64, 256], P('prompt', 'resp')
- prefix_key_grad: bfloat16 [8, 512, 256], P('prompt', 'resp')
- prefix_value_grad: bfloat16 [8, 512, 256], P('prompt', 'resp')
- router_grad: float32 [2048, 128], replicated
- gain_grad: float32 [2048], replicated
- gate_grad: bfloat16 [128, 2048, 768], P(('prompt', 'resp'))
- up_grad: bfloat16 [128, 2048, 768], P(('prompt', 'resp'))
- down_grad: bfloat16 [128, 768, 2048], P(('prompt', 'resp'))
Inputs may be any that keep to these rules, and one draw needn't show every extreme that they name: `expert_ids`: among the rows of one device no expert is named by more than 6 rows, a bound that some block reaches; the experts of a row differ. `lengths`: every prompt has a response of 64 positions.
All inputs are finite; a program needn't handle non-finite values.
Results may differ from a plain program's by a relative error of at most 0.039.
Values may be sent and summed in bfloat16 or wider, within the bound.
No kernel may reach another device: no remote copies, remote signals or barrier semaphores. Data moves between devices by JAX's collectives and lax.ppermute only.
A program may use at most 192 MiB of HBM per device.

v0:
```python
import jax
import jax.numpy as jnp
from jax import lax
from jax.sharding import PartitionSpec as P

QUERY_HEADS = 16
KEY_VALUE_HEADS = 2
HEAD_SIZE = 128


def silu_parts(pre_gate):
    sigmoid = jax.nn.sigmoid(pre_gate)
    return (pre_gate * sigmoid, sigmoid * (1.0 + pre_gate * (1.0 - sigmoid)))


def allowed_keys(span_length, prompt_prefix):
    row_pos = jnp.arange(span_length)[:, None]
    col_pos = jnp.arange(prompt_prefix + span_length)[None, :]
    return (col_pos < prompt_prefix) | (col_pos - prompt_prefix <= row_pos)


def prompt_attention(query_matrix, key_matrix, value_matrix, prompt_key_rows, prompt_value_rows):
    item_count = query_matrix.shape[0]
    span_length = query_matrix.shape[1]
    prompt_prefix = prompt_key_rows.shape[0]
    group_index = QUERY_HEADS // KEY_VALUE_HEADS
    query_quintet = query_matrix.reshape(
        item_count, span_length, KEY_VALUE_HEADS, group_index, HEAD_SIZE
    )
    joined_keys = jnp.concatenate(
        [
            jnp.broadcast_to(
                prompt_key_rows.reshape(1, prompt_prefix, KEY_VALUE_HEADS, HEAD_SIZE),
                (item_count, prompt_prefix, KEY_VALUE_HEADS, HEAD_SIZE),
            ),
            key_matrix.reshape(item_count, span_length, KEY_VALUE_HEADS, HEAD_SIZE),
        ],
        axis=1,
    )
    joined_values = jnp.concatenate(
        [
            jnp.broadcast_to(
                prompt_value_rows.reshape(1, prompt_prefix, KEY_VALUE_HEADS, HEAD_SIZE),
                (item_count, prompt_prefix, KEY_VALUE_HEADS, HEAD_SIZE),
            ),
            value_matrix.reshape(item_count, span_length, KEY_VALUE_HEADS, HEAD_SIZE),
        ],
        axis=1,
    )
    scores = jnp.einsum(
        "blkgd,bskd->bkgls", query_quintet, joined_keys, preferred_element_type=jnp.float32
    ) * HEAD_SIZE ** (-0.5)
    scores = jnp.where(allowed_keys(span_length, prompt_prefix), scores, -jnp.inf)
    attn_probs = jax.nn.softmax(scores, axis=-1)
    probs_low = attn_probs.astype(jnp.bfloat16)
    attn_out = jnp.einsum(
        "bkgls,bskd->blkgd", probs_low, joined_values, preferred_element_type=jnp.float32
    ).astype(jnp.bfloat16)
    return (
        query_quintet,
        joined_keys,
        joined_values,
        attn_probs,
        probs_low,
        attn_out.reshape(item_count * span_length, QUERY_HEADS * HEAD_SIZE),
    )


def attention_back(
    query_quintet, joined_keys, joined_values, attn_probs, probs_low, attention_gradient
):
    item_count = query_quintet.shape[0]
    span_length = query_quintet.shape[1]
    gradient_quintet = attention_gradient.reshape(
        item_count, span_length, KEY_VALUE_HEADS, QUERY_HEADS // KEY_VALUE_HEADS, HEAD_SIZE
    )
    prob_back = jnp.einsum(
        "blkgd,bskd->bkgls", gradient_quintet, joined_values, preferred_element_type=jnp.float32
    )
    delta = jnp.sum(attn_probs * prob_back, axis=-1, keepdims=True)
    score_back = (attn_probs * (prob_back - delta) * HEAD_SIZE ** (-0.5)).astype(jnp.bfloat16)
    query_grad = jnp.einsum(
        "bkgls,bskd->blkgd", score_back, joined_keys, preferred_element_type=jnp.float32
    ).astype(jnp.bfloat16)
    key_gradient = jnp.einsum(
        "bkgls,blkgd->bskd", score_back, query_quintet, preferred_element_type=jnp.float32
    )
    value_gradient = jnp.einsum(
        "bkgls,blkgd->bskd", probs_low, gradient_quintet, preferred_element_type=jnp.float32
    )
    return (query_grad, key_gradient, value_gradient)


def shards(
    queries,
    response_keys,
    response_values,
    prefix_keys,
    prompt_values,
    resid,
    out_proj,
    router,
    norm_gain,
    w_gate,
    w_up,
    w_down,
    expert_ids,
    lengths,
    out_grad,
):
    item_count = queries.shape[1]
    span_length = queries.shape[2]
    width = resid.shape[3]
    experts = router.shape[1]
    top_count = expert_ids.shape[3]
    dev_rows = item_count * span_length
    copies = dev_rows * top_count
    capacity = max(2, 3 * dev_rows * top_count // (2 * experts))
    contract_one = (((1,), (1,)), ((), ()))
    contract_zero = (((0,), (0,)), ((), ()))

    def route(block):
        moved = lax.all_to_all(
            block.reshape(experts, capacity, width),
            ("prompt", "resp"),
            split_axis=0,
            concat_axis=0,
            tiled=True,
        )
        return moved.reshape(experts * capacity, width)

    near_keys, near_values = (
        lax.all_gather(prefix_keys, "resp", axis=1, tiled=True),
        lax.all_gather(prompt_values, "resp", axis=1, tiled=True),
    )
    prompt_prefix = near_keys.shape[1]
    query_quintet, joined_keys, joined_values, attn_probs, probs_low, attn_flat = prompt_attention(
        queries[0], response_keys[0], response_values[0], near_keys[0], near_values[0]
    )
    mixed = jnp.dot(
        attn_flat,
        lax.all_gather(out_proj, "prompt", axis=0, tiled=True),
        preferred_element_type=jnp.float32,
    )
    xmid = resid.reshape(dev_rows, width).astype(jnp.float32) + mixed
    rinv = lax.rsqrt(jnp.mean(xmid * xmid, axis=-1, keepdims=True) + 1e-06)
    normed = xmid * rinv
    hidden = (normed * norm_gain).astype(jnp.bfloat16)
    logits = jnp.dot(hidden, router, preferred_element_type=jnp.float32)
    ids = expert_ids.reshape(dev_rows, top_count)
    chosen = jnp.exp(jnp.take_along_axis(logits, ids, axis=1))
    gates = chosen / jnp.sum(chosen, axis=1, keepdims=True)
    flat_ids = ids.reshape(copies)
    onehot = (flat_ids[:, None] == jnp.arange(experts, dtype=jnp.int32)[None, :]).astype(jnp.int32)
    slot = jnp.sum(jnp.cumsum(onehot, axis=0) * onehot, axis=1) - 1
    dest = flat_ids * capacity + slot
    source = (
        jnp.full((experts * capacity,), copies, jnp.int32)
        .at[dest]
        .set(jnp.arange(copies, dtype=jnp.int32))
    )
    hidden_pad = jnp.concatenate([hidden, jnp.zeros((1, width), jnp.bfloat16)], axis=0)
    expert_in = route(hidden_pad[source // top_count])
    gate_e = w_gate[0]
    up_e = w_up[0]
    down_e = w_down[0]
    pre_gate = jnp.dot(expert_in, gate_e, preferred_element_type=jnp.float32)
    pre_up = jnp.dot(expert_in, up_e, preferred_element_type=jnp.float32)
    silu_value, silu_slope = silu_parts(pre_gate)
    act = (silu_value * pre_up).astype(jnp.bfloat16)
    expert_out = jnp.dot(act, down_e, preferred_element_type=jnp.float32).astype(jnp.bfloat16)
    out_copies = route(expert_out)[dest].reshape(dev_rows, top_count, width)
    layer_out = (
        xmid + jnp.einsum("rk,rkd->rd", gates, out_copies, preferred_element_type=jnp.float32)
    ).astype(jnp.bfloat16)
    live = (jnp.arange(span_length, dtype=jnp.int32)[None, :] < lengths[0][:, None]).reshape(
        dev_rows, 1
    )
    grad = jnp.where(live, out_grad.reshape(dev_rows, width).astype(jnp.float32), 0.0)
    copy_grad = (gates[:, :, None] * grad[:, None, :]).astype(jnp.bfloat16)
    gate_back = jnp.einsum("rd,rkd->rk", grad, out_copies, preferred_element_type=jnp.float32)
    grad_pad = jnp.concatenate(
        [copy_grad.reshape(copies, width), jnp.zeros((1, width), jnp.bfloat16)], axis=0
    )
    out_back = route(grad_pad[source])
    act_back = lax.dot_general(out_back, down_e, contract_one, preferred_element_type=jnp.float32)
    down_part = lax.dot_general(
        act, out_back, contract_zero, preferred_element_type=jnp.float32
    ).astype(jnp.bfloat16)
    pre_back = (act_back * pre_up * silu_slope).astype(jnp.bfloat16)
    up_back = (act_back * silu_value).astype(jnp.bfloat16)
    gate_part = lax.dot_general(
        expert_in, pre_back, contract_zero, preferred_element_type=jnp.float32
    ).astype(jnp.bfloat16)
    up_part = lax.dot_general(
        expert_in, up_back, contract_zero, preferred_element_type=jnp.float32
    ).astype(jnp.bfloat16)
    input_back = (
        lax.dot_general(pre_back, gate_e, contract_one, preferred_element_type=jnp.float32)
        + lax.dot_general(up_back, up_e, contract_one, preferred_element_type=jnp.float32)
    ).astype(jnp.bfloat16)
    back_copies = route(input_back)[dest].reshape(dev_rows, top_count, width)
    hidden_back = jnp.sum(back_copies.astype(jnp.float32), axis=1)
    route_back = gates * (gate_back - jnp.sum(gates * gate_back, axis=1, keepdims=True))
    picked = ids[:, :, None] == jnp.arange(experts, dtype=jnp.int32)[None, None, :]
    logit_back = jnp.sum(jnp.where(picked, route_back[:, :, None], 0.0), axis=1).astype(
        jnp.bfloat16
    )
    router_part = lax.dot_general(
        hidden, logit_back, contract_zero, preferred_element_type=jnp.float32
    )
    hidden_back = hidden_back + lax.dot_general(
        logit_back, router, contract_one, preferred_element_type=jnp.float32
    )
    gain_part = jnp.sum(hidden_back * normed, axis=0)
    router_grad, gain_grad = lax.psum((router_part, gain_part), ("prompt", "resp"))
    norm_back = hidden_back * norm_gain
    xmid_back = grad + rinv * (
        norm_back - normed * jnp.mean(norm_back * normed, axis=-1, keepdims=True)
    )
    resid_grad = xmid_back.astype(jnp.bfloat16)
    attention_gradient = lax.dot_general(
        resid_grad,
        lax.all_gather(out_proj, "prompt", axis=0, tiled=True),
        contract_one,
        preferred_element_type=jnp.float32,
    )
    attention_gradient = attention_gradient.astype(jnp.bfloat16)
    query_grad, key_gradient, value_gradient = attention_back(
        query_quintet, joined_keys, joined_values, attn_probs, probs_low, attention_gradient
    )
    prompt_key_portion = jnp.sum(key_gradient[:, :prompt_prefix], axis=0).reshape(
        prompt_prefix, KEY_VALUE_HEADS * HEAD_SIZE
    )
    prompt_value_portion = jnp.sum(value_gradient[:, :prompt_prefix], axis=0).reshape(
        prompt_prefix, KEY_VALUE_HEADS * HEAD_SIZE
    )
    prompt_key_gradient, prompt_value_gradient = (
        lax.psum_scatter(
            prompt_key_portion.astype(jnp.bfloat16), "resp", scatter_dimension=0, tiled=True
        ).astype(jnp.float32),
        lax.psum_scatter(
            prompt_value_portion.astype(jnp.bfloat16), "resp", scatter_dimension=0, tiled=True
        ).astype(jnp.float32),
    )
    local_key_gradient = (
        key_gradient[:, prompt_prefix:]
        .astype(jnp.bfloat16)
        .reshape(1, item_count, span_length, KEY_VALUE_HEADS * HEAD_SIZE)
    )
    local_value_gradient = (
        value_gradient[:, prompt_prefix:]
        .astype(jnp.bfloat16)
        .reshape(1, item_count, span_length, KEY_VALUE_HEADS * HEAD_SIZE)
    )
    partition_rows = prompt_key_gradient.shape[0]
    return (
        layer_out.reshape(1, item_count, span_length, width),
        resid_grad.reshape(1, item_count, span_length, width),
        query_grad.reshape(1, item_count, span_length, QUERY_HEADS * HEAD_SIZE),
        local_key_gradient,
        local_value_gradient,
        prompt_key_gradient.astype(jnp.bfloat16).reshape(
            1, partition_rows, KEY_VALUE_HEADS * HEAD_SIZE
        ),
        prompt_value_gradient.astype(jnp.bfloat16).reshape(
            1, partition_rows, KEY_VALUE_HEADS * HEAD_SIZE
        ),
        router_grad,
        gain_grad,
        gate_part[None],
        up_part[None],
        down_part[None],
    )


def solution(mesh):
    in_specs = (
        P("prompt", "resp", None, None),
        P("prompt", "resp", None, None),
        P("prompt", "resp", None, None),
        P("prompt", "resp", None),
        P("prompt", "resp", None),
        P("prompt", "resp", None, None),
        P("prompt", None),
        P(),
        P(),
        P(("prompt", "resp"), None, None),
        P(("prompt", "resp"), None, None),
        P(("prompt", "resp"), None, None),
        P("prompt", "resp", None, None),
        P("prompt", "resp"),
        P("prompt", "resp", None, None),
    )
    out_specs = (
        P("prompt", "resp", None, None),
        P("prompt", "resp", None, None),
        P("prompt", "resp", None, None),
        P("prompt", "resp", None, None),
        P("prompt", "resp", None, None),
        P("prompt", "resp", None),
        P("prompt", "resp", None),
        P(),
        P(),
        P(("prompt", "resp"), None, None),
        P(("prompt", "resp"), None, None),
        P(("prompt", "resp"), None, None),
    )
    return jax.shard_map(shards, mesh=mesh, in_specs=in_specs, out_specs=out_specs, check_vma=False)
```

profile of v0, /device:TPU:1, one launch (start us, length us, event | category | flops | bytes accessed | tf_op | source)
XLA Modules:
  0.0 717.0 jit_solution(17688806847142848359)
XLA Ops:
  9.1 28.3 %all_gather.11 = bf16[1,512,256]{2,1,0:T(8,128)(2,1)} all-gather(bf16[1,32,256]{2,1,0:T(8,128)(2,1)} %param.18), channel_id=1, replica_groups=mesh['prompt'=8,'resp'=16] {'resp'}, dimensions={1}, use_global_device_ids=true | all-gather | bytes 278528 | tf_op jit(solution)/shard_map/all_gather | solution.py:133
  41.2 20.5 %all_gather.10 = bf16[1,512,256]{2,1,0:T(8,128)(2,1)S(1)} all-gather(bf16[1,32,256]{2,1,0:T(8,128)(2,1)} %param.19), channel_id=1, replica_groups=mesh['prompt'=8,'resp'=16] {'resp'}, dimensions={1}, use_global_device_ids=true | all-gather | bytes 278528 | tf_op jit(solution)/shard_map/all_gather | solution.py:134
  83.2 24.2 %all-gather.2.cloned.1.call-done = bf16[2048,2048]{1,0:T(8,128)(2,1)} async-done(((bf16[256,2048]{1,0:T(8,128)(2,1)}), bf16[2048,2048]{1,0:T(8,128)(2,1)}) %all-gather.2.cloned.1.call-update) | async-done | bytes 8388624 | tf_op jit(solution)/shard_map/all_gather | solution.py:142
  115.1 8.2 %gather_fusion = bf16[768,2048]{1,0:T(8,128)(2,1)} fusion(bf16[129,2048]{1,0:T(8,128)(2,1)} %concatenate.14, s32[1024]{0:T(1024)S(1)} %get-tuple-element.77), kind=kCustom, calls=%fused_computation | custom fusion | bytes 6294528 | tf_op jit(solution)/shard_map/gather | solution.py:163
  123.3 6.2 reshape.286
  156.4 9.0 %gather_fusion.2 = bf16[768,2048]{1,0:T(8,128)(2,1)} fusion(bf16[513,2048]{1,0:T(8,128)(2,1)} %concatenate.15, s32[1024]{0:T(1024)S(1)} %get-tuple-element.76), kind=kCustom, calls=%fused_computation.2 | custom fusion | bytes 6294528 | tf_op jit(solution)/shard_map/gather | solution.py:185
  165.4 6.3 reshape.292
  171.7 16.3 %all-to-all-done = bf16[128,6,2048]{2,1,0:T(8,128)(2,1)} async-done(((bf16[128,6,2048]{2,1,0:T(8,128)(2,1)}), bf16[128,6,2048]{2,1,0:T(8,128)(2,1)}, u32[]{:S(2)}, u32[]{:S(2)}) %all-to-all-start) | async-done | bytes 3145760 | tf_op jit(solution)/shard_map/all_to_all | solution.py:123
  188.0 7.6 %all-to-all-start.2 = ((bf16[128,6,2048]{2,1,0:T(8,128)(2,1)}), bf16[128,6,2048]{2,1,0:T(8,128)(2,1)}, u32[]{:S(2)}, u32[]{:S(2)}) async-start(bf16[128,6,2048]{2,1,0:T(8,128)(2,1)} %reshape.292), calls=%async_computation.2 | async-start | bytes 8388608 | tf_op jit(solution)/shard_map/all_to_all | solution.py:123
  195.6 6.3 reshape.287
  202.0 7.0 fusion.10
  213.0 34.9 %all-to-all-done.2 = bf16[128,6,2048]{2,1,0:T(8,128)(2,1)} async-done(((bf16[128,6,2048]{2,1,0:T(8,128)(2,1)}), bf16[128,6,2048]{2,1,0:T(8,128)(2,1)}, u32[]{:S(2)}, u32[]{:S(2)}) %all-to-all-start.2) | async-done | bytes 3145760 | tf_op jit(solution)/shard_map/all_to_all | solution.py:123
  247.9 6.3 reshape.293
  254.2 8.1 %multiply_convert_fusion.1 = (bf16[768,768]{1,0:T(8,128)(2,1)}, bf16[768,768]{1,0:T(8,128)(2,1)}, bf16[768,768]{1,0:T(8,128)(2,1)S(1)}) fusion(f32[768,768]{1,0:T(8,128)} %fusion.14, f32[768,768]{1,0:T(8,128)} %fusion.10, bf16[768,2048]{1,0:T(8,128)(2,1)} %reshape.293, bf16[1,768,2048]{2,1,0:T(8,128)(2,1)S(1)} %copy-done), kind=kOutput, calls=%fused_computation.44 | convolution fusion | flops 2424766464 | bytes 14548992 | tf_op jit(solution)/shard_map/dot_general | solution.py:186
  273.6 7.4 %all-to-all-start.1 = ((bf16[128,6,2048]{2,1,0:T(8,128)(2,1)}), bf16[128,6,2048]{2,1,0:T(8,128)(2,1)}, u32[]{:S(2)}, u32[]{:S(2)}) async-start(bf16[128,6,2048]{2,1,0:T(8,128)(2,1)} %reshape.288), calls=%async_computation.1 | async-start | bytes 8388608 | tf_op jit(solution)/shard_map/all_to_all | solution.py:123
  290.8 42.4 %all-to-all-done.1 = bf16[128,6,2048]{2,1,0:T(8,128)(2,1)} async-done(((bf16[128,6,2048]{2,1,0:T(8,128)(2,1)}), bf16[128,6,2048]{2,1,0:T(8,128)(2,1)}, u32[]{:S(2)}, u32[]{:S(2)}) %all-to-all-start.1) | async-done | bytes 3145760 | tf_op jit(solution)/shard_map/all_to_all | solution.py:123
  333.2 7.0 all-to-all-start.3
  362.4 30.3 %all-to-all-done.3 = bf16[128,6,2048]{2,1,0:T(8,128)(2,1)} async-done(((bf16[128,6,2048]{2,1,0:T(8,128)(2,1)}), bf16[128,6,2048]{2,1,0:T(8,128)(2,1)}, u32[]{:S(2)}, u32[]{:S(2)}) %all-to-all-start.3) | async-done | bytes 3145760 | tf_op jit(solution)/shard_map/all_to_all | solution.py:123
  413.8 6.6 fusion.35
  428.8 19.9 %fusion.28 = f32[2,576,2,128]{3,1,2,0:T(8,128)S(1)} fusion(f32[2,2,576,64,8]{2,3,4,1,0:T(8,128)} %fusion.39, bf16[2,64,2,8,128]{4,3,2,1,0:T(8,128)(2,1)S(1)} %bitcast.193, f32[2,2,8,64,576]{4,3,2,1,0:T(8,128)} %copy-done.8, f32[2,2,8,64]{3,2,1,0:T(8,128)S(1)} %copy-done.28), kind=kOutput, calls=%fused_computation.52 | convolution fusion | flops 310250048 | bytes 11149312 | tf_op jit(solution)/shard_map/bkgls,blkgd->bskd/dot_general | solution.py:85
  457.6 6.6 fusion.17
  466.7 16.2 %fusion.34 = bf16[2,64,2,8,128]{4,1,3,2,0:T(8,128)(2,1)} fusion(f32[2,2,576,64,8]{2,3,4,1,0:T(8,128)} %fusion.39, bf16[2,64,2,128]{3,1,2,0:T(8,128)(2,1)S(1)} %copy-done.23, bf16[2,512,2,128]{3,1,2,0:T(8,128)(2,1)} %copy-done.17, f32[2,2,8,64,576]{4,3,2,1,0:T(8,128)} %copy-done.8, f32[2,2,8,64]{3,2,1,0:T(8,128)S(1)} %copy-done.28), kind=kOutput, calls=%fused_computation.57 | convolution fusion | flops 311691840 | bytes 10559488 | tf_op jit(solution)/shard_map/bkgls,bskd->blkgd/dot_general | solution.py:82
  487.1 65.5 %psum.15 = f32[2048]{0:T(1024)} all-reduce(f32[2048]{0:T(1024)S(1)} %get-tuple-element.60), channel_id=1, replica_groups=mesh['prompt'=8,'resp'=16] {'prompt','resp'}, use_global_device_ids=true, to_apply=%region_19.20 | all-reduce | flops 2048 | bytes 16384 | tf_op jit(solution)/shard_map/psum | solution.py:216
  555.7 152.1 %all-reduce.4.cloned.1.call-done = f32[2048,128]{1,0:T(8,128)} async-done(((f32[2048,128]{1,0:T(8,128)}), f32[2048,128]{1,0:T(8,128)}) %all-reduce.4.cloned.1.call-update) | async-done | bytes 1048592 | tf_op jit(solution)/shard_map/psum | solution.py:216
  (201 shorter events, 158.9 us)
Async XLA Ops:
  7.2 247.0 %copy-start = (bf16[1,768,2048]{2,1,0:T(8,128)(2,1)S(1)}, bf16[1,768,2048]{2,1,0:T(8,128)(2,1)}, u32[]{:S(2)}) copy-start(bf16[1,768,2048]{2,1,0:T(8,128)(2,1)} %param.26) | copy-start | bytes 9437188
  7.2 33.9 %copy-start.26 = (bf16[1,2,64,256]{3,2,1,0:T(8,128)(2,1)S(1)}, bf16[1,2,64,256]{3,2,1,0:T(8,128)(2,1)}, u32[]{:S(2)}) copy-start(bf16[1,2,64,256]{3,2,1,0:T(8,128)(2,1)} %param.16) | copy-start | bytes 196612
  7.2 100.1 %all-gather.2.cloned.1.call-start = ((), (), s32[]{:S(2)}) async-start(), calls=%async_computation.6 | async-start | bytes 9437184 | tf_op jit(solution)/shard_map/all_gather | solution.py:142
  41.2 28.4 %copy-start.22 = (bf16[2,64,2,128]{3,1,2,0:T(8,128)(2,1)}, bf16[2,64,2,128]{3,1,2,0:T(8,128)(2,1)S(1)}, u32[]{:S(2)}) copy-start(bf16[2,64,2,128]{3,1,2,0:T(8,128)(2,1)S(1)} %copy.195) | copy-start | bytes 196612
  107.3 6.0 copy-start.24
  129.6 6.3 copy-start.32
  129.6 58.4 %all-to-all-start = ((bf16[128,6,2048]{2,1,0:T(8,128)(2,1)}), bf16[128,6,2048]{2,1,0:T(8,128)(2,1)}, u32[]{:S(2)}, u32[]{:S(2)}) async-start(bf16[128,6,2048]{2,1,0:T(8,128)(2,1)} %reshape.286), calls=%async_computation | async-start | bytes 8388608 | tf_op jit(solution)/shard_map/all_to_all | solution.py:123
  188.0 59.9 %all-to-all-start.2 = ((bf16[128,6,2048]{2,1,0:T(8,128)(2,1)}), bf16[128,6,2048]{2,1,0:T(8,128)(2,1)}, u32[]{:S(2)}, u32[]{:S(2)}) async-start(bf16[128,6,2048]{2,1,0:T(8,128)(2,1)} %reshape.292), calls=%async_computation.2 | async-start | bytes 8388608 | tf_op jit(solution)/shard_map/all_to_all | solution.py:123
  202.0 7.0 copy-start.15
  202.0 7.0 copy-start.29
  273.6 7.4 %copy-start.30 = (bf16[1,2048,768]{2,1,0:T(8,128)(2,1)S(1)}, bf16[1,2048,768]{2,1,0:T(8,128)(2,1)}, u32[]{:S(2)}) copy-start(bf16[1,2048,768]{2,1,0:T(8,128)(2,1)} %param.24) | copy-start | bytes 9437188
  273.6 59.7 %all-to-all-start.1 = ((bf16[128,6,2048]{2,1,0:T(8,128)(2,1)}), bf16[128,6,2048]{2,1,0:T(8,128)(2,1)}, u32[]{:S(2)}, u32[]{:S(2)}) async-start(bf16[128,6,2048]{2,1,0:T(8,128)(2,1)} %reshape.288), calls=%async_computation.1 | async-start | bytes 8388608 | tf_op jit(solution)/shard_map/all_to_all | solution.py:123
  290.8 49.8 %copy-start.16 = (bf16[768,2048]{1,0:T(8,128)(2,1)S(1)}, bf16[768,2048]{1,0:T(8,128)(2,1)}, u32[]{:S(2)}) copy-start(bf16[768,2048]{1,0:T(8,128)(2,1)} %reshape.293) | copy-start | bytes 9437188
  333.2 59.5 %all-to-all-start.3 = ((bf16[128,6,2048]{2,1,0:T(8,128)(2,1)}), bf16[128,6,2048]{2,1,0:T(8,128)(2,1)}, u32[]{:S(2)}, u32[]{:S(2)}) async-start(bf16[128,6,2048]{2,1,0:T(8,128)(2,1)} %reshape.294), calls=%async_computation.3 | async-start | bytes 8388608 | tf_op jit(solution)/shard_map/all_to_all | solution.py:123
  340.3 212.3 %reduce-scatter.9.cloned.1.call-start = ((), (), s32[]{:S(2)}) async-start(), calls=%async_computation.9 | async-start | bytes 278528
  405.8 4.9 copy-start.5
  413.8 6.6 copy-start.19
  413.8 6.7 copy-start.3
  424.5 129.7 %reduce-scatter.7.cloned.1.call-start = ((), (), s32[]{:S(2)}) async-start(), calls=%async_computation.8 | async-start | bytes 278528
  428.8 21.3 %copy-start.33 = (bf16[768,768]{1,0:T(8,128)(2,1)S(1)}, bf16[768,768]{1,0:T(8,128)(2,1)}, u32[]{:S(2)}) copy-start(bf16[768,768]{1,0:T(8,128)(2,1)} %get-tuple-element.65) | copy-start | bytes 3538948
  449.7 6.6 copy-start.7
  449.7 258.1 %all-reduce.4.cloned.1.call-start = ((), (), s32[]{:S(2)}) async-start(), calls=%async_computation.7 | async-start | bytes 2097152 | tf_op jit(solution)/shard_map/psum | solution.py:216
  457.6 9.1 %copy-start.23 = (bf16[2,64,2,128]{3,1,2,0:T(8,128)(2,1)S(1)}, bf16[2,64,2,128]{3,1,2,0:T(8,128)(2,1)}, u32[]{:S(2)}) copy-start(bf16[2,64,2,128]{3,1,2,0:T(8,128)(2,1)} %copy-done.22) | copy-start | bytes 196612
  466.7 243.4 %copy-start.1 = (bf16[1,768,2048]{2,1,0:T(8,128)(2,1)S(1)}, bf16[1,768,2048]{2,1,0:T(8,128)(2,1)}, u32[]{:S(2)}) copy-start(bf16[1,768,2048]{2,1,0:T(8,128)(2,1)} %param.26) | copy-start | bytes 9437188
  (20 other events, 46.0 us)
Sparse Core Ops, SparseCore 0:
  9.7 97.6 all-gather.1
  424.6 61.3 reduce-scatter.8
  490.2 63.9 reduce-scatter.6
  559.4 148.3 all-reduce.3
where the time goes:
time: 728 us; the launch traced here: 717 us
  waiting for transfers between devices  301 us (41%)
  local copies, waits for them, and re-layouts  131 us (18%)
  blocking collectives  114 us (16%)
  matrix products  114 us (16%)
  starting transfers between devices  28.5 us (4%)
  between operations  15 us (2%)
  other arithmetic  13.9 us (2%)
    psum x1, waiting for transfers between devices, shards(): lax.psum((router_part, gain_part), ('prompt', 'resp'))  152 us
    all_to_all x4, waiting for transfers between devices, route(): lax.all_to_all(block.reshape(experts, capacity, width), ('prompt', 'resp'...  124 us
    psum x1, blocking collectives, shards(): lax.psum((router_part, gain_part), ('prompt', 'resp'))  65.5 us
    all_gather x1, blocking collectives, shards(): lax.all_gather(prefix_keys, 'resp', axis=1, tiled=True)  28.3 us
    all_to_all x4, starting transfers between devices, route(): lax.all_to_all(block.reshape(experts, capacity, width), ('prompt', 'resp'...  28 us
    all_gather x1, waiting for transfers between devices, shards(): lax.all_gather(out_proj, 'prompt', axis=0, tiled=True)  24.2 us
    reshape x4, local copies, waits for them, and re-layouts, route(): return moved.reshape(experts * capacity, width)  22.4 us
    reshape x4, local copies, waits for them, and re-layouts, route(): block.reshape(experts, capacity, width)  21.6 us
  transfers between devices with their start and end apart: 8, of which 7 were waited for; matrix products, arithmetic and copies ran while one was open for 24% of the time, Pallas kernels for 0%

commit v1 on v0

v1 whole, which is shorter than its diff:
```python
import jax
import jax.numpy as jnp
from jax import lax
from jax.experimental import pallas as pl
from jax.experimental.pallas import tpu as pltpu
from jax.sharding import PartitionSpec as P

D = 2048
HEADS = 16
KV = 2
GROUP = HEADS // KV
HS = 128
FF = 768
TOPK = 4
PREFIX = 512
SPAN = 64
ROWS = 128
EXPERTS = 128
CAP = 6
N_PROMPT = 8
N_RESP = 16
DEVICES = 128
SLOTS = DEVICES * CAP
PACKED = DEVICES * 8
MAIN = 1536
TAIL = 512
EXTRA = 128
SCALE = HS ** (-0.5)
BF = jnp.bfloat16
F32 = jnp.float32
MIB = 1024 * 1024


def mm(a, b):
    return jnp.dot(a, b, preferred_element_type=F32)


def mm_nt(a, b):
    return lax.dot_general(a, b, (((1,), (1,)), ((), ())), preferred_element_type=F32)


def mm_tn(a, b):
    return lax.dot_general(a, b, (((0,), (0,)), ((), ())), preferred_element_type=F32)


def iota(shape, dim):
    return lax.broadcasted_iota(jnp.int32, shape, dim)


def chosen_by_row(ids):
    lanes = iota((ROWS, EXPERTS), 1)
    hit = ids[:, 0:1] == lanes
    for k in range(1, TOPK):
        hit = hit | (ids[:, k : k + 1] == lanes)
    return hit


def chosen_by_expert(ids_t):
    subs = iota((EXPERTS, ROWS), 0)
    hit = ids_t[0:1, :] == subs
    for k in range(1, TOPK):
        hit = hit | (ids_t[k : k + 1, :] == subs)
    return hit


def to_bf(mask):
    return jnp.where(mask, 1.0, 0.0).astype(BF)


def packed_slots(ids_t):
    hit = chosen_by_expert(ids_t)
    before = to_bf(iota((ROWS, ROWS), 0) < iota((ROWS, ROWS), 1))
    slot = mm(to_bf(hit), before)
    slot = jnp.where(hit, slot, -1.0).astype(BF)
    spread = to_bf((iota((PACKED, EXPERTS), 0) >> 3) == iota((PACKED, EXPERTS), 1))
    return mm(spread, slot).astype(jnp.int32)


def packed_slots_by_row(ids):
    hit = chosen_by_row(ids)
    before = to_bf(iota((ROWS, ROWS), 1) < iota((ROWS, ROWS), 0))
    slot = mm(before, to_bf(hit))
    slot = jnp.where(hit, slot, -1.0).astype(BF)
    spread = to_bf(iota((EXPERTS, PACKED), 0) == (iota((EXPERTS, PACKED), 1) >> 3))
    return mm(slot, spread).astype(jnp.int32)


def selectors(slot, place):
    head = to_bf((slot == place) & (place < CAP))
    tails = [to_bf((slot == place * 3 - 18 + j) & (place >= CAP)) for j in range(3)]
    return head, tails


def pack_rows(rows, head, tails, out_ref):
    last = rows[:, MAIN:]
    for j in range(3):
        select = jnp.concatenate([head, tails[j]], axis=1)
        both = jnp.concatenate([rows[:, j * TAIL : (j + 1) * TAIL], last], axis=0)
        out_ref[:, j * TAIL : (j + 1) * TAIL] = mm(select, both).astype(BF)


def combine(head, tails, packed_ref):
    pieces = [mm(head, packed_ref[:, j * TAIL : (j + 1) * TAIL]) for j in range(3)]
    last = mm(tails[0], packed_ref[:, 0:TAIL])
    for j in range(1, 3):
        last = last + mm(tails[j], packed_ref[:, j * TAIL : (j + 1) * TAIL])
    return pieces + [last]


def static_selectors(by_slot):
    shape, slot_dim = ((96, 128), 0) if by_slot else ((128, 96), 1)
    slot = iota(shape, slot_dim)
    packed = iota(shape, 1 - slot_dim)
    place = packed & 7
    base = (packed >> 3) * CAP
    head = to_bf((slot == base + place) & (place < CAP))
    tails = [to_bf((slot == base + place * 3 - 18 + j) & (place >= CAP)) for j in range(3)]
    return head, tails


def grad_pack_kernel(ids_t_ref, ids_ref, live_ref, grad_ref, out_ref):
    slot = packed_slots(ids_t_ref[...])
    head, tails = selectors(slot, iota((PACKED, ROWS), 0) & 7)
    grad = jnp.where(live_ref[...] > 0, grad_ref[...].astype(F32), 0.0).astype(BF)
    pack_rows(grad, head, tails, out_ref)
    out_ref[:, MAIN:] = mm(head, to_bf(chosen_by_row(ids_ref[...]))).astype(BF)


def allowed_own():
    key = iota((ROWS, ROWS), 0)
    row = iota((ROWS, ROWS), 1)
    return ((key >> 6) == (row >> 6)) & ((key & 63) <= (row & 63))


def attention_kernel(q_ref, rk_ref, rv_ref, prefix_ref, out_ref, lse_ref):
    mask = allowed_own()
    for kv in range(KV):
        lanes = slice(kv * HS, (kv + 1) * HS)
        vlanes = slice((KV + kv) * HS, (KV + kv + 1) * HS)
        keys = jnp.concatenate([prefix_ref[:, lanes], rk_ref[:, lanes]], axis=0)
        values = jnp.concatenate([prefix_ref[:, vlanes], rv_ref[:, lanes]], axis=0)
        values_t = values.astype(F32).T.astype(BF)
        for g in range(GROUP):
            h = kv * GROUP + g
            cols = slice(h * HS, (h + 1) * HS)
            scores = mm_nt(keys, q_ref[:, cols]) * SCALE
            near = jnp.where(mask, scores[PREFIX:], -1e30)
            scores = jnp.concatenate([scores[:PREFIX], near], axis=0)
            top = jnp.max(scores, axis=0, keepdims=True)
            probs = jnp.exp(scores - top)
            total = jnp.sum(probs, axis=0, keepdims=True)
            low = (probs * (1.0 / total)).astype(BF)
            out_ref[:, cols] = mm(values_t, low).T.astype(BF)
            lse_ref[h : h + 1, :] = top + jnp.log(total)


def project_kernel(
    core_ref, attn_ref, attn_other_ref, w_ref, w_other_ref, resid_ref, gain_ref, router_ref, ids_ref, ids_t_ref, xmid_ref, hidden_ref, gates_ref, out_ref
):
    step = pl.program_id(0)
    attn = jnp.concatenate([attn_ref[...], attn_other_ref[...]], axis=1)
    part = mm(attn, jnp.concatenate([w_ref[...], w_other_ref[...]], axis=0))

    @pl.when(step == 0)
    def _():
        xmid_ref[...] = resid_ref[...].astype(F32) + part

    @pl.when(step > 0)
    def _():
        xmid_ref[...] += part

    @pl.when(step == pl.num_programs(0) - 1)
    def _():
        xmid = xmid_ref[...]
        rinv = lax.rsqrt(jnp.mean(xmid * xmid, axis=-1, keepdims=True) + 1e-06)
        hidden = (xmid * rinv * gain_ref[...]).astype(BF)
        hidden_ref[...] = hidden
        slot = packed_slots(ids_t_ref[...])
        head, tails = selectors(slot, iota((PACKED, ROWS), 0) & 7)
        pack_rows(hidden, head, tails, out_ref)
        logits = mm(hidden, router_ref[...])
        chosen = jnp.where(chosen_by_row(ids_ref[...]), jnp.exp(logits), 0.0)
        gates_ref[...] = chosen / jnp.sum(chosen, axis=1, keepdims=True)


def expert_kernel(
    own_ref, router_ref, x_ref, g_ref, wg_hbm, wu_hbm, wd_hbm,
    back_hbm, out_hbm, xc_hbm, ob_hbm, act_hbm, pb_hbm, ub_hbm,
    wg, wu, wd, xc, ob, act, pb, ub, pg, pu, outs, back8, out8, in_sem, out_sem,
):
    copies = [
        pltpu.make_async_copy(src, dst, in_sem.at[i])
        for i, (src, dst) in enumerate(((wg_hbm, wg), (wu_hbm, wu), (wd_hbm, wd)))
    ]
    for copy in copies:
        copy.start()
    stores = [
        pltpu.make_async_copy(src, dst, out_sem.at[i])
        for i, (src, dst) in enumerate(
            ((xc, xc_hbm), (act, act_hbm), (ob, ob_hbm), (out8, out_hbm), (pb, pb_hbm), (ub, ub_hbm), (back8, back_hbm))
        )
    ]

    head, tails = static_selectors(True)
    tail3 = jnp.concatenate(tails, axis=1)

    def unpack(block, src, dst):
        rows = pl.ds(pl.multiple_of(block * 128, 128), 128)
        to = pl.ds(pl.multiple_of(block * 96, 32), 96)
        part = src[rows, 0:MAIN]
        dst[to, 0:MAIN] = mm(head, part).astype(BF)
        stacked = jnp.concatenate([part[:, j * TAIL : (j + 1) * TAIL] for j in range(3)], axis=0)
        dst[to, MAIN:] = mm(tail3, stacked).astype(BF)

    @pl.loop(0, 8)
    def _(block):
        unpack(block, x_ref, xc)

    stores[0].start()
    copies[0].wait()
    copies[1].wait()

    @pl.loop(0, 3)
    def _(n):
        cols = pl.ds(pl.multiple_of(n * 256, 256), 256)
        gate = mm(xc[...], wg[:, cols])
        up = mm(xc[...], wu[:, cols])
        pg[:, cols] = gate
        pu[:, cols] = up
        act[:, cols] = (gate * jax.nn.sigmoid(gate) * up).astype(BF)

    stores[1].start()

    @pl.loop(0, 8)
    def _(block):
        unpack(block, g_ref, ob)

    mask = jnp.concatenate([mm(head, g_ref[i * 128 : (i + 1) * 128, MAIN:]) for i in range(8)], axis=0)
    own_hi = own_ref[0:1, :]
    own_lo = own_ref[1:2, :]
    logits = mm(xc[...], router_ref[...])
    chosen = jnp.where(mask > 0.5, jnp.exp(logits), 0.0)
    total = jnp.sum(chosen, axis=1, keepdims=True)
    own = jnp.sum(chosen * own_hi, axis=1, keepdims=True)
    gate_col = jnp.where(total > 0.0, own / jnp.where(total > 0.0, total, 1.0), 0.0)

    copies[2].wait()

    def out_tile(n, gate_back):
        cols = pl.ds(pl.multiple_of(n * 256, 256), 256)
        value = mm(act[...], wd[:, cols]).astype(BF).astype(F32)
        raw = ob[:, cols].astype(F32)
        outs[:, cols] = (gate_col * value).astype(BF)
        ob[:, cols] = (gate_col * raw).astype(BF)
        both = value * raw
        return gate_back + both[:, 0:128] + both[:, 128:256]

    gate_back = lax.fori_loop(0, 8, out_tile, jnp.zeros((SLOTS, 128), F32))
    stores[2].start()
    gate_back = jnp.sum(gate_back, axis=1, keepdims=True)
    back_hi = gate_back.astype(BF).astype(F32)
    extra = (back_hi * own_hi + (gate_back - back_hi) * own_lo).astype(BF)

    @pl.loop(0, 3)
    def _(n):
        cols = pl.ds(pl.multiple_of(n * 256, 256), 256)
        act_back = mm_nt(ob[...], wd[cols, :])
        gate = pg[:, cols]
        sig = jax.nn.sigmoid(gate)
        pb[:, cols] = (act_back * pu[:, cols] * (sig * (1.0 + gate * (1.0 - sig)))).astype(BF)
        ub[:, cols] = (act_back * (gate * sig)).astype(BF)

    stores[4].start()
    stores[5].start()

    head_t, tails_t = static_selectors(False)
    selects = [jnp.concatenate([head_t, tail], axis=1) for tail in tails_t]

    def pack(block, src, dst):
        rows = pl.ds(pl.multiple_of(block * 128, 128), 128)
        at = pl.ds(pl.multiple_of(block * 96, 32), 96)
        last = src[at, MAIN:]
        for j in range(3):
            both = jnp.concatenate([src[at, j * TAIL : (j + 1) * TAIL], last], axis=0)
            dst[rows, j * TAIL : (j + 1) * TAIL] = mm(selects[j], both).astype(BF)

    @pl.loop(0, 8)
    def _(block):
        pack(block, outs, out8)

    stores[3].start()

    @pl.loop(0, 8)
    def _(n):
        cols = pl.ds(pl.multiple_of(n * 256, 256), 256)
        outs[:, cols] = (mm_nt(pb[...], wg[cols, :]) + mm_nt(ub[...], wu[cols, :])).astype(BF)

    @pl.loop(0, 8)
    def _(block):
        pack(block, outs, back8)

    for i in range(8):
        back8[i * 128 : (i + 1) * 128, MAIN:] = mm(head_t, extra[i * 96 : (i + 1) * 96]).astype(BF)
    stores[6].start()
    for store in stores:
        store.wait()


def weight_grad_kernel(xc_ref, ob_ref, act_ref, pb_ref, ub_ref, gate_ref, up_ref, down_ref, act_t):
    @pl.when(pl.program_id(0) == 0)
    def _():
        act_t[...] = act_ref[...].astype(F32).T.astype(BF)

    xt = xc_ref[...].astype(F32).T.astype(BF)
    gate_ref[...] = mm(xt, pb_ref[...]).astype(BF)
    up_ref[...] = mm(xt, ub_ref[...]).astype(BF)
    down_ref[...] = mm(act_t[...], ob_ref[...]).astype(BF)


def back_kernel(
    core_ref, back_ref, xmid_ref, hidden_ref, gates_ref, grad_ref, live_ref, ids_ref, gain_ref, router_ref, w_ref, w_other_ref,
    resid_ref, sums_ref, attn_back_ref, acc,
):
    @pl.when(pl.program_id(0) == 0)
    def _():
        slot = packed_slots_by_row(ids_ref[...])
        head, tails = selectors(slot, iota((ROWS, PACKED), 1) & 7)
        pieces = combine(head, tails, back_ref)
        expert = iota((PACKED, EXPERTS), 0) >> 3
        lane = iota((PACKED, EXPERTS), 1)
        extra = back_ref[:, MAIN:].astype(F32)
        hi = mm(head, jnp.where(lane == expert, extra, 0.0).astype(BF))
        lo = mm(head, jnp.where(lane == ((expert + 64) & 127), extra, 0.0).astype(BF))
        gate_back = hi + pltpu.roll(lo, 64, 1)
        gates = gates_ref[...]
        route = gates * (gate_back - jnp.sum(gates * gate_back, axis=1, keepdims=True))
        logit_back = route.astype(BF)
        sums_ref[:, 0:EXPERTS] = mm_tn(hidden_ref[...], logit_back).astype(BF)
        xmid = xmid_ref[...]
        rinv = lax.rsqrt(jnp.mean(xmid * xmid, axis=-1, keepdims=True) + 1e-06)
        ones = jnp.ones((ROWS, EXPERTS), BF)
        mean = jnp.zeros((ROWS, 1), F32)
        for j in range(4):
            cols = slice(j * TAIL, (j + 1) * TAIL)
            value = pieces[j] + mm_nt(logit_back, router_ref[cols, :])
            normed = xmid[:, cols] * rinv
            sums_ref[cols, EXPERTS:] = mm_tn((value * normed).astype(BF), ones).astype(BF)
            value = value * gain_ref[:, cols]
            acc[:, cols] = value
            mean = mean + jnp.sum(value * normed, axis=-1, keepdims=True)
        mean = mean * (1.0 / D)
        grad = jnp.where(live_ref[...] > 0, grad_ref[...].astype(F32), 0.0)
        resid_ref[...] = (grad + rinv * (acc[...] - xmid * rinv * mean)).astype(BF)

    first = core_ref[0] == 0
    near, far = w_ref[...], w_other_ref[...]
    half = near.shape[0]
    value = mm_nt(resid_ref[...], jnp.concatenate([near, far], axis=0)).astype(BF)

    @pl.when(first)
    def _():
        attn_back_ref[...] = value

    @pl.when(jnp.logical_not(first))
    def _():
        attn_back_ref[:, 0:half] = value[:, half:]
        attn_back_ref[:, half:] = value[:, 0:half]


def attention_back_kernel(q_ref, rk_ref, rv_ref, prefix_ref, lse_ref, ab_ref, dq_ref, dk_ref, dv_ref, dprefix_ref, ds_all, p_all):
    mask = allowed_own()
    for kv in range(KV):
        lanes = slice(kv * HS, (kv + 1) * HS)
        vlanes = slice((KV + kv) * HS, (KV + kv + 1) * HS)
        keys = jnp.concatenate([prefix_ref[:, lanes], rk_ref[:, lanes]], axis=0)
        values = jnp.concatenate([prefix_ref[:, vlanes], rv_ref[:, lanes]], axis=0)
        keys_t = keys.astype(F32).T.astype(BF)
        q_parts = []
        ab_parts = []
        for g in range(GROUP):
            h = kv * GROUP + g
            cols = slice(h * HS, (h + 1) * HS)
            q = q_ref[:, cols]
            ab = ab_ref[:, cols]
            q_parts.append(q)
            ab_parts.append(ab)
            scores = mm_nt(keys, q) * SCALE
            near = jnp.where(mask, scores[PREFIX:], -1e30)
            scores = jnp.concatenate([scores[:PREFIX], near], axis=0)
            probs = jnp.exp(scores - lse_ref[h : h + 1, :])
            prob_back = mm_nt(values, ab)
            delta = jnp.sum(probs * prob_back, axis=0, keepdims=True)
            score_back = (probs * (prob_back - delta) * SCALE).astype(BF)
            at = slice(g * ROWS, (g + 1) * ROWS)
            p_all[:, at] = probs.astype(BF)
            ds_all[:, at] = score_back
            dq_ref[:, cols] = mm(keys_t, score_back).T.astype(BF)
        dk = mm(ds_all[...], jnp.concatenate(q_parts, axis=0)).astype(BF)
        dv = mm(p_all[...], jnp.concatenate(ab_parts, axis=0)).astype(BF)
        dprefix_ref[:, lanes] = dk[:PREFIX]
        dprefix_ref[:, vlanes] = dv[:PREFIX]
        dk_ref[:, lanes] = dk[PREFIX:]
        dv_ref[:, lanes] = dv[PREFIX:]


def layer_out_kernel(out8_ref, xmid_ref, ids_ref, out_ref):
    slot = packed_slots_by_row(ids_ref[...])
    head, tails = selectors(slot, iota((ROWS, PACKED), 1) & 7)
    pieces = combine(head, tails, out8_ref)
    for j in range(4):
        cols = slice(j * TAIL, (j + 1) * TAIL)
        out_ref[:, cols] = (xmid_ref[:, cols] + pieces[j]).astype(BF)


def struct(shape, dtype):
    return jax.ShapeDtypeStruct(shape, dtype)


def params(limit):
    return pltpu.CompilerParams(vmem_limit_bytes=limit * MIB)


def cost(flops, moved):
    return pl.CostEstimate(flops=int(flops), bytes_accessed=int(moved), transcendentals=0)


VMEM_SPEC = pl.BlockSpec(memory_space=pltpu.VMEM)
ANY_SPEC = pl.BlockSpec(memory_space=pl.ANY)


def whole(shape):
    return pl.BlockSpec(shape, lambda *at: (0,) * len(shape))


def exchange(block, width):
    moved = lax.all_to_all(
        block.reshape(DEVICES, 8, width), ("prompt", "resp"), split_axis=0, concat_axis=0, tiled=True
    )
    return moved.reshape(PACKED, width)


def shards(
    queries, response_keys, response_values, prefix_keys, prompt_values, resid, out_proj, router, norm_gain,
    w_gate, w_up, w_down, expert_ids, lengths, out_grad,
):
    p_at = lax.axis_index("prompt")
    r_at = lax.axis_index("resp")
    me = p_at * N_RESP + r_at
    lane = jnp.arange(EXPERTS, dtype=jnp.int32)
    own = jnp.stack([lane == me] + [lane == (me + 64) % EXPERTS] * 7).astype(F32)
    ids = expert_ids.reshape(ROWS, TOPK)
    ids_t = ids.T
    live = (jnp.arange(SPAN, dtype=jnp.int32)[None, :] < lengths[0][:, None]).astype(F32).reshape(ROWS, 1)
    grad = out_grad.reshape(ROWS, D)
    q = queries.reshape(ROWS, D)
    rk = response_keys.reshape(ROWS, KV * HS)
    rv = response_values.reshape(ROWS, KV * HS)
    gain = norm_gain.reshape(1, D)

    prefix_part = jnp.concatenate([prefix_keys[0], prompt_values[0]], axis=1)
    prefix = lax.all_to_all(
        jnp.broadcast_to(prefix_part[None], (N_RESP,) + prefix_part.shape), "resp", split_axis=0, concat_axis=0, tiled=True
    ).reshape(PREFIX, 2 * KV * HS)
    piece = D // DEVICES
    half = D // N_PROMPT // 2
    core = r_at % 2
    w_own = lax.dynamic_slice(out_proj, (core * half, 0), (half, D))
    w_own = lax.all_gather(w_own, "prompt", axis=0, tiled=True)
    w_other = lax.ppermute(w_own, "resp", [(i, i ^ 1) for i in range(N_RESP)])
    core = core.astype(jnp.int32).reshape(1)

    grad8 = pl.pallas_call(
        grad_pack_kernel,
        out_shape=struct((PACKED, MAIN + EXTRA), BF),
        in_specs=[VMEM_SPEC] * 4,
        out_specs=VMEM_SPEC,
        compiler_params=params(32),
        cost_estimate=cost(1.2e9, 4e6),
        name="grad_pack",
    )(ids_t, ids, live, grad)
    grad8 = exchange(grad8, MAIN + EXTRA)

    attn, lse = pl.pallas_call(
        attention_kernel,
        out_shape=(struct((ROWS, D), BF), struct((HEADS, ROWS), F32)),
        in_specs=[VMEM_SPEC] * 4,
        out_specs=(VMEM_SPEC, VMEM_SPEC),
        compiler_params=params(32),
        cost_estimate=cost(4e9, 2e6),
        name="attention",
    )(q, rk, rv, prefix)

    steps = N_PROMPT
    xmid, hidden, gates, x8 = pl.pallas_call(
        project_kernel,
        grid_spec=pltpu.PrefetchScalarGridSpec(
            num_scalar_prefetch=1,
            grid=(steps,),
            in_specs=[
                pl.BlockSpec((ROWS, half), lambda i, c: (0, 2 * i + c[0])),
                pl.BlockSpec((ROWS, half), lambda i, c: (0, 2 * i + 1 - c[0])),
                pl.BlockSpec((half, D), lambda i, c: (i, 0)),
                pl.BlockSpec((half, D), lambda i, c: (i, 0)),
                whole((ROWS, D)), whole((1, D)), whole((D, EXPERTS)), whole((ROWS, TOPK)), whole((TOPK, ROWS)),
            ],
            out_specs=(whole((ROWS, D)), whole((ROWS, D)), whole((ROWS, EXPERTS)), whole((PACKED, MAIN))),
        ),
        out_shape=(
            struct((ROWS, D), F32), struct((ROWS, D), BF), struct((ROWS, EXPERTS), F32), struct((PACKED, MAIN), BF)
        ),
        compiler_params=params(40),
        cost_estimate=cost(3e9, 14e6),
        name="project",
    )(core, attn, attn, w_own, w_other, resid.reshape(ROWS, D), gain, router, ids, ids_t)
    x8 = exchange(x8, MAIN)

    back8, out8, xc, ob, act, pb, ub = pl.pallas_call(
        expert_kernel,
        out_shape=(
            struct((PACKED, MAIN + EXTRA), BF), struct((PACKED, MAIN), BF), struct((SLOTS, D), BF),
            struct((SLOTS, D), BF), struct((SLOTS, FF), BF), struct((SLOTS, FF), BF), struct((SLOTS, FF), BF),
        ),
        in_specs=[VMEM_SPEC] * 4 + [ANY_SPEC] * 3,
        out_specs=(ANY_SPEC,) * 7,
        scratch_shapes=[
            pltpu.VMEM((D, FF), BF), pltpu.VMEM((D, FF), BF), pltpu.VMEM((FF, D), BF),
            pltpu.VMEM((SLOTS, D), BF), pltpu.VMEM((SLOTS, D), BF),
            pltpu.VMEM((SLOTS, FF), BF), pltpu.VMEM((SLOTS, FF), BF), pltpu.VMEM((SLOTS, FF), BF),
            pltpu.VMEM((SLOTS, FF), F32), pltpu.VMEM((SLOTS, FF), F32),
            pltpu.VMEM((SLOTS, D), BF), pltpu.VMEM((PACKED, MAIN + EXTRA), BF), pltpu.VMEM((PACKED, MAIN), BF),
            pltpu.SemaphoreType.DMA((3,)), pltpu.SemaphoreType.DMA((7,)),
        ],
        compiler_params=params(58),
        cost_estimate=cost(16e9, 32e6),
        name="expert",
    )(own, router, x8, grad8, w_gate[0], w_up[0], w_down[0])
    back8 = exchange(back8, MAIN + EXTRA)
    out8 = exchange(out8, MAIN)

    gate_grad, up_grad, down_grad = pl.pallas_call(
        weight_grad_kernel,
        grid=(8,),
        out_shape=(struct((D, FF), BF), struct((D, FF), BF), struct((FF, D), BF)),
        in_specs=[
            pl.BlockSpec((SLOTS, 256), lambda i: (0, i)), pl.BlockSpec((SLOTS, 256), lambda i: (0, i)),
            whole((SLOTS, FF)), whole((SLOTS, FF)), whole((SLOTS, FF)),
        ],
        out_specs=(
            pl.BlockSpec((256, FF), lambda i: (i, 0)), pl.BlockSpec((256, FF), lambda i: (i, 0)),
            pl.BlockSpec((FF, 256), lambda i: (0, i)),
        ),
        scratch_shapes=[pltpu.VMEM((FF, SLOTS), BF)],
        compiler_params=params(32),
        cost_estimate=cost(7.3e9, 20e6),
        name="weight_grad",
    )(xc, ob, act, pb, ub)

    resid_grad, sums, attn_back = pl.pallas_call(
        back_kernel,
        grid_spec=pltpu.PrefetchScalarGridSpec(
            num_scalar_prefetch=1,
            grid=(steps,),
            in_specs=[
                whole((PACKED, MAIN + EXTRA)), whole((ROWS, D)), whole((ROWS, D)), whole((ROWS, EXPERTS)),
                whole((ROWS, D)), whole((ROWS, 1)), whole((ROWS, TOPK)), whole((1, D)), whole((D, EXPERTS)),
                pl.BlockSpec((half, D), lambda i, c: (i, 0)),
                pl.BlockSpec((half, D), lambda i, c: (i, 0)),
            ],
            out_specs=(
                whole((ROWS, D)), whole((D, 2 * EXPERTS)), pl.BlockSpec((ROWS, 2 * half), lambda i, c: (0, i))
            ),
            scratch_shapes=[pltpu.VMEM((ROWS, D), F32)],
        ),
        out_shape=(struct((ROWS, D), BF), struct((D, 2 * EXPERTS), BF), struct((ROWS, D), BF)),
        compiler_params=params(48),
        cost_estimate=cost(3e9, 16e6),
        name="back",
    )(core, back8, xmid, hidden, gates, grad, live, ids, gain, router, w_own, w_other)

    query_grad, resp_key_grad, resp_value_grad, prefix_grad = pl.pallas_call(
        attention_back_kernel,
        out_shape=(
            struct((ROWS, D), BF), struct((ROWS, KV * HS), BF), struct((ROWS, KV * HS), BF),
            struct((PREFIX, 2 * KV * HS), BF),
        ),
        in_specs=[VMEM_SPEC] * 6,
        out_specs=(VMEM_SPEC,) * 4,
        scratch_shapes=[pltpu.VMEM((PREFIX + ROWS, GROUP * ROWS), BF)] * 2,
        compiler_params=params(32),
        cost_estimate=cost(8e9, 4e6),
        name="attention_back",
    )(q, rk, rv, prefix, lse, attn_back)

    prefix_grad = lax.all_to_all(
        prefix_grad.reshape(N_RESP, PREFIX // N_RESP, 2 * KV * HS), "resp", split_axis=0, concat_axis=0, tiled=True
    )
    prefix_grad = jnp.sum(prefix_grad.astype(F32), axis=0).astype(BF)

    sums = lax.all_to_all(
        sums.reshape(DEVICES, piece, 2 * EXPERTS), ("prompt", "resp"), split_axis=0, concat_axis=0, tiled=True
    )
    sums = jnp.sum(sums.astype(F32), axis=0).astype(BF)
    sums = lax.all_to_all(
        jnp.broadcast_to(sums[None], (DEVICES, piece, 2 * EXPERTS)),
        ("prompt", "resp"), split_axis=0, concat_axis=0, tiled=True,
    ).reshape(D, 2 * EXPERTS)

    layer_out = pl.pallas_call(
        layer_out_kernel,
        out_shape=struct((ROWS, D), BF),
        in_specs=[VMEM_SPEC] * 3,
        out_specs=VMEM_SPEC,
        compiler_params=params(32),
        cost_estimate=cost(1e9, 5e6),
        name="layer_out",
    )(out8, xmid, ids)

    rows_shape = (1, ROWS // SPAN, SPAN, D)
    near_shape = (1, ROWS // SPAN, SPAN, KV * HS)
    return (
        layer_out.reshape(rows_shape),
        resid_grad.reshape(rows_shape),
        query_grad.reshape(rows_shape),
        resp_key_grad.reshape(near_shape),
        resp_value_grad.reshape(near_shape),
        prefix_grad[None, :, : KV * HS],
        prefix_grad[None, :, KV * HS :],
        sums[:, :EXPERTS].astype(F32),
        sums[:, EXPERTS].astype(F32),
        gate_grad[None],
        up_grad[None],
        down_grad[None],
    )


def solution(mesh):
    in_specs = (
        P("prompt", "resp", None, None),
        P("prompt", "resp", None, None),
        P("prompt", "resp", None, None),
        P("prompt", "resp", None),
        P("prompt", "resp", None),
        P("prompt", "resp", None, None),
        P("prompt", None),
        P(),
        P(),
        P(("prompt", "resp"), None, None),
        P(("prompt", "resp"), None, None),
        P(("prompt", "resp"), None, None),
        P("prompt", "resp", None, None),
        P("prompt", "resp"),
        P("prompt", "resp", None, None),
    )
    out_specs = (
        P("prompt", "resp", None, None),
        P("prompt", "resp", None, None),
        P("prompt", "resp", None, None),
        P("prompt", "resp", None, None),
        P("prompt", "resp", None, None),
        P("prompt", "resp", None),
        P("prompt", "resp", None),
        P(),
        P(),
        P(("prompt", "resp"), None, None),
        P(("prompt", "resp"), None, None),
        P(("prompt", "resp"), None, None),
    )
    return jax.shard_map(shards, mesh=mesh, in_specs=in_specs, out_specs=out_specs, check_vma=False)
```

time: 728 us -> 399 us (0.55); the launches traced: 717 us -> 397 us
  waiting for transfers between devices: 301 us -> 175 us
  matrix products: 114 us -> 0 us
  local copies, waits for them, and re-layouts: 131 us -> 24 us
  Pallas kernels: 0 us -> 85.6 us
  blocking collectives: 114 us -> 50 us
  starting transfers between devices: 28.5 us -> 40 us
    psum x1 -> x0, waiting for transfers between devices: 152 us -> none  [shards(): lax.psum((router_part, gain_part), ('prompt', 'resp'))]
    dot_general x22 -> x0, matrix products: 114 us -> none  [the longest x1 19.9 us: attention_back(): jnp.einsum('bkgls,blkgd->bskd', score_back, query_quintet, preferred_elem...]
    pallas_call x0 -> x8, Pallas kernels: none -> 85.6 us  [the longest x1 35.7 us: shards(): pl.pallas_call(expert_kernel, out_shape=(struct((PACKED, MAIN + EXTRA), B...]
    psum x1 -> x0, blocking collectives: 65.5 us -> none  [shards(): lax.psum((router_part, gain_part), ('prompt', 'resp'))]
    reshape x15 -> x0, local copies, waits for them, and re-layouts: 52.4 us -> none  [the longest x4 22.4 us: route(): return moved.reshape(experts * capacity, width)]
    all_to_all x0 -> x1, blocking collectives: none -> 50 us  [exchange(): lax.all_to_all(block.reshape(DEVICES, 8, width), ('prompt', 'resp'), spli...]
    all_gather x2 -> x0, blocking collectives: 48.8 us -> none  [the longest x1 28.3 us: shards(): lax.all_gather(prefix_keys, 'resp', axis=1, tiled=True)]
    all_gather x1, waiting for transfers between devices: 24.2 us -> 57.1 us  [shards(): w_own = lax.all_gather(w_own, 'prompt', axis=0, tiled=True)]
  transfers between devices with their start and end apart: 8 -> 9, of which waited for: 7 -> 7; matrix products, arithmetic and copies ran while one was open for 24% -> 1% of each run, Pallas kernels for 0% -> 13%
where the time goes in v1:
time: 399 us; the launch traced here: 397 us
  waiting for transfers between devices  175 us (44%)
  Pallas kernels  85.6 us (21%)
  blocking collectives  50 us (13%)
  starting transfers between devices  40 us (10%)
  local copies, waits for them, and re-layouts  24 us (6%)
  between operations  14.4 us (4%)
  other arithmetic  7.89 us (2%)
    all_to_all x3, waiting for transfers between devices, exchange(): lax.all_to_all(block.reshape(DEVICES, 8, width), ('prompt', 'resp'), spli...  93.3 us
    all_gather x1, waiting for transfers between devices, shards(): w_own = lax.all_gather(w_own, 'prompt', axis=0, tiled=True)  57.1 us
    all_to_all x1, blocking collectives, exchange(): lax.all_to_all(block.reshape(DEVICES, 8, width), ('prompt', 'resp'), spli...  50 us
    pallas_call x1, Pallas kernels, shards(): pl.pallas_call(expert_kernel, out_shape=(struct((PACKED, MAIN + EXTRA), B...  35.7 us
    unnamed x69, local copies, waits for them, and re-layouts  20.4 us
    all_to_all x3, starting transfers between devices, exchange(): lax.all_to_all(block.reshape(DEVICES, 8, width), ('prompt', 'resp'), spli...  16.3 us
    pallas_call x1, Pallas kernels, shards(): pl.pallas_call(back_kernel, grid_spec=pltpu.PrefetchScalarGridSpec(num_sc...  12.5 us
    pallas_call x1, Pallas kernels, shards(): pl.pallas_call(weight_grad_kernel, grid=(8,), out_shape=(struct((D, FF),...  11.3 us
  transfers between devices with their start and end apart: 9, of which 7 were waited for; matrix products, arithmetic and copies ran while one was open for 1% of the time, Pallas kernels for 13%

profile of v1, /device:TPU:1, one launch (start us, length us, event | category | flops | bytes accessed | tf_op | source)
XLA Modules:
  0.0 397.3 jit_solution(17670628041685340205)
XLA Ops:
  9.3 57.1 %all-gather.2.cloned.1.call-done.w_ref = bf16[1024,2048]{1,0:T(8,128)(2,1)} async-done(((bf16[128,2048]{1,0:T(8,128)(2,1)}), bf16[1024,2048]{1,0:T(8,128)(2,1)}) %all-gather.2.cloned.1.call-update) | async-done | bytes 4194320 | tf_op jit(solution)/shard_map/all_gather | solution.py:468
  68.6 6.5 %all-to-all-start = ((bf16[16,32,512]{2,1,0:T(8,128)(2,1)}), bf16[16,32,512]{2,1,0:T(8,128)(2,1)S(1)}, u32[]{:S(2)}, u32[]{:S(2)}) async-start(bf16[16,32,512]{2,1,0:T(8,128)(2,1)} %broadcast_in_dim.28), calls=%async_computation | async-start | bytes 1048576 | tf_op jit(solution)/shard_map/all_to_all | solution.py:461
  75.5 3.2 grad_pack.1
  78.8 7.7 %all-to-all-done = bf16[16,32,512]{2,1,0:T(8,128)(2,1)S(1)} async-done(((bf16[16,32,512]{2,1,0:T(8,128)(2,1)}), bf16[16,32,512]{2,1,0:T(8,128)(2,1)S(1)}, u32[]{:S(2)}, u32[]{:S(2)}) %all-to-all-start) | async-done | bytes 524320 | tf_op jit(solution)/shard_map/all_to_all | solution.py:461
  86.5 5.7 %all-to-all-start.2 = ((bf16[128,8,1664]{2,1,0:T(8,128)(2,1)}), bf16[128,8,1664]{2,1,0:T(8,128)(2,1)}, u32[]{:S(2)}, u32[]{:S(2)}) async-start(bf16[128,8,1664]{2,1,0:T(8,128)(2,1)} %bitcast.15), calls=%async_computation.2 | async-start | bytes 6815744 | tf_op jit(solution)/shard_map/all_to_all | solution.py:436
  92.3 2.8 attention.1
  95.2 9.9 %project.1 = (f32[128,2048]{1,0:T(8,128)S(1)}, bf16[128,2048]{1,0:T(8,128)(2,1)S(1)}, f32[128,128]{1,0:T(8,128)S(1)}, bf16[1024,1536]{1,0:T(8,128)(2,1)}) custom-call(s32[1]{0:T(128)} %bitcast.core_ref, bf16[128,2048]{1,0:T(8,128)(2,1)S(1)} %get-tuple-element.35.attn_ref.attn_other_ref, bf16[128,2048]{1,0:T(8,128)(2,1)S(1)} %get-tuple-element.35.attn_ref.attn_other_ref, ...), custom_call_target="tpu_custom_call" | custom-call | flops 3000000000 | bytes 14000000 | tf_op jit(solution)/shard_map/project/pallas_call | solution.py:494
  106.9 29.5 %all-to-all-done.2 = bf16[128,8,1664]{2,1,0:T(8,128)(2,1)} async-done(((bf16[128,8,1664]{2,1,0:T(8,128)(2,1)}), bf16[128,8,1664]{2,1,0:T(8,128)(2,1)}, u32[]{:S(2)}, u32[]{:S(2)}) %all-to-all-start.2) | async-done | bytes 3407904 | tf_op jit(solution)/shard_map/all_to_all | solution.py:436
  136.4 5.3 %all-to-all-start.1 = ((bf16[128,8,1536]{2,1,0:T(8,128)(2,1)}), bf16[128,8,1536]{2,1,0:T(8,128)(2,1)S(1)}, u32[]{:S(2)}, u32[]{:S(2)}) async-start(bf16[128,8,1536]{2,1,0:T(8,128)(2,1)} %bitcast.11), calls=%async_computation.1 | async-start | bytes 6291456 | tf_op jit(solution)/shard_map/all_to_all | solution.py:436
  142.4 40.8 %all-to-all-done.1 = bf16[128,8,1536]{2,1,0:T(8,128)(2,1)S(1)} async-done(((bf16[128,8,1536]{2,1,0:T(8,128)(2,1)}), bf16[128,8,1536]{2,1,0:T(8,128)(2,1)S(1)}, u32[]{:S(2)}, u32[]{:S(2)}) %all-to-all-start.1) | async-done | bytes 3145760 | tf_op jit(solution)/shard_map/all_to_all | solution.py:436
  184.9 35.7 %expert.1 = (bf16[1024,1664]{1,0:T(8,128)(2,1)}, bf16[1024,1536]{1,0:T(8,128)(2,1)}, bf16[768,2048]{1,0:T(8,128)(2,1)}, bf16[768,2048]{1,0:T(8,128)(2,1)}, bf16[...) custom-call(f32[8,128]{1,0:T(8,128)} %convert_element_type.29.own_ref, ...), custom_call_target="tpu_custom_call" | custom-call | flops 16000000000 | bytes 32000000 | tf_op jit(solution)/shard_map/expert/pallas_call | solution.py:517
  220.6 50.0 %all_to_all.40 = bf16[128,8,1664]{2,1,0:T(8,128)(2,1)} all-to-all(bf16[128,8,1664]{2,1,0:T(8,128)(2,1)} %bitcast.62), channel_id=1, replica_groups=mesh['prompt'=8,'resp'=16] {'prompt','resp'}, dimensions={0} | all-to-all | bytes 6815744 | tf_op jit(solution)/shard_map/all_to_all | solution.py:436
  270.6 5.3 %all-to-all-start.3 = ((bf16[128,8,1536]{2,1,0:T(8,128)(2,1)}), bf16[128,8,1536]{2,1,0:T(8,128)(2,1)S(1)}, u32[]{:S(2)}, u32[]{:S(2)}) async-start(bf16[128,8,1536]{2,1,0:T(8,128)(2,1)} %bitcast.64), calls=%async_computation.3 | async-start | bytes 6291456 | tf_op jit(solution)/shard_map/all_to_all | solution.py:436
  280.3 12.5 %back.1 = (bf16[128,2048]{1,0:T(8,128)(2,1)}, bf16[2048,256]{1,0:T(8,128)(2,1)S(1)}, bf16[128,2048]{1,0:T(8,128)(2,1)S(1)}) custom-call(s32[1]{0:T(128)} %bitcast.core_ref, bf16[1024,1664]{1,0:T(8,128)(2,1)} %bitcast.61, f32[128,2048]{1,0:T(8,128)S(1)} %copy-done.6, bf16[128,2048]{1,0:T(8,128)(2,1)S(1)} %copy-done.14, ...), custom_call_target="tpu_custom_call" | custom-call | flops 3000000000 | bytes 16000000 | tf_op jit(solution)/shard_map/back/pallas_call | solution.py:558
  294.5 22.9 %all-to-all-done.3 = bf16[128,8,1536]{2,1,0:T(8,128)(2,1)S(1)} async-done(((bf16[128,8,1536]{2,1,0:T(8,128)(2,1)}), bf16[128,8,1536]{2,1,0:T(8,128)(2,1)S(1)}, u32[]{:S(2)}, u32[]{:S(2)}) %all-to-all-start.3) | async-done | bytes 3145760 | tf_op jit(solution)/shard_map/all_to_all | solution.py:436
  317.4 5.7 %all-to-all-start.6 = ((bf16[128,16,256]{2,1,0:T(8,128)(2,1)}), bf16[128,16,256]{2,1,0:T(8,128)(2,1)}, u32[]{:S(2)}, u32[]{:S(2)}) async-start(bf16[128,16,256]{2,1,0:T(8,128)(2,1)} %bitcast.46), calls=%async_computation.6 | async-start | bytes 2097152 | tf_op jit(solution)/shard_map/all_to_all | solution.py:599
  326.3 8.0 %attention_back.1 = (bf16[128,2048]{1,0:T(8,128)(2,1)}, bf16[128,256]{1,0:T(8,128)(2,1)}, bf16[128,256]{1,0:T(8,128)(2,1)}, bf16[512,512]{1,0:T(8,128)(2,1)S(1)}) custom-call(bf16[128,2048]{1,0:T(8,128)(2,1)S(1)} %bitcast.56, bf16[128,256]{1,0:T(8,128)(2,1)S(1)} %bitcast.58, bf16[128,256]{1,0:T(8,128)(2,1)S(1)} %bitcast.60, bf16[512,512]{1,0:T(8,128)(2,1)S(1)} %bitcast.50, ...), custom_call_target="tpu_custom_call" | custom-call | flops 8000000000 | bytes 4000000 | tf_op jit(solution)/shard_map/attention_back/pallas_call | solution.py:580
  335.1 7.0 %all-to-all-done.6 = bf16[128,16,256]{2,1,0:T(8,128)(2,1)} async-done(((bf16[128,16,256]{2,1,0:T(8,128)(2,1)}), bf16[128,16,256]{2,1,0:T(8,128)(2,1)}, u32[]{:S(2)}, u32[]{:S(2)}) %all-to-all-start.6) | async-done | bytes 1048608 | tf_op jit(solution)/shard_map/all_to_all | solution.py:599
  342.1 5.2 %all-to-all-start.5 = ((bf16[16,32,512]{2,1,0:T(8,128)(2,1)}), bf16[16,32,512]{2,1,0:T(8,128)(2,1)}, u32[]{:S(2)}, u32[]{:S(2)}) async-start(bf16[16,32,512]{2,1,0:T(8,128)(2,1)} %bitcast.51), calls=%async_computation.5 | async-start | bytes 1048576 | tf_op jit(solution)/shard_map/all_to_all | solution.py:594
  348.8 10.2 %all-to-all-done.5 = bf16[16,32,512]{2,1,0:T(8,128)(2,1)} async-done(((bf16[16,32,512]{2,1,0:T(8,128)(2,1)}), bf16[16,32,512]{2,1,0:T(8,128)(2,1)}, u32[]{:S(2)}, u32[]{:S(2)}) %all-to-all-start.5) | async-done | bytes 524320 | tf_op jit(solution)/shard_map/all_to_all | solution.py:594
  360.0 5.5 %all-to-all-start.7 = ((bf16[128,16,256]{2,1,0:T(8,128)(2,1)}), bf16[128,16,256]{2,1,0:T(8,128)(2,1)}, u32[]{:S(2)}, u32[]{:S(2)}) async-start(bf16[128,16,256]{2,1,0:T(8,128)(2,1)} %broadcast_in_dim.31), calls=%async_computation.7 | async-start | bytes 2097152 | tf_op jit(solution)/shard_map/all_to_all | solution.py:603
  371.3 11.3 %weight_grad.1 = (bf16[2048,768]{1,0:T(8,128)(2,1)}, bf16[2048,768]{1,0:T(8,128)(2,1)}, bf16[768,2048]{1,0:T(8,128)(2,1)}) custom-call(bf16[768,2048]{1,0:T(8,128)(2,1)S(1)} %copy-done.26, bf16[768,2048]{1,0:T(8,128)(2,1)S(1)} %copy-done.27, bf16[768,768]{1,0:T(8,128)(2,1)S(1)} %copy-done.28, bf16[768,768]{1,0:T(8,128)(2,1)S(1)} %copy-done.29, ...), custom_call_target="tpu_custom_call" | custom-call | flops 7299999744 | bytes 20000000 | tf_op jit(solution)/shard_map/weight_grad/pallas_call | solution.py:540
  382.6 2.2 layer_out.1
  388.4 2.1 slice_convert_fusion
  (88 shorter events, 30.6 us)
Async XLA Ops:
  7.2 67.9 %copy-start.33 = (s32[1,2]{1,0:T(1,128)S(1)}, s32[1,2]{1,0:T(1,128)}, u32[]{:S(2)}) copy-start(s32[1,2]{1,0:T(1,128)} %param.28) | copy-start | bytes 28
  7.2 68.2 %copy-start.32 = (s32[1,2,64,4]{2,3,1,0:T(4,128)S(1)}, s32[1,2,64,4]{2,3,1,0:T(4,128)}, u32[]{:S(2)}) copy-start(s32[1,2,64,4]{2,3,1,0:T(4,128)} %param.27) | copy-start | bytes 6148
  7.2 68.3 %copy-start.11 = (bf16[1,2,64,2048]{3,2,1,0:T(8,128)(2,1)S(1)}, bf16[1,2,64,2048]{3,2,1,0:T(8,128)(2,1)}, u32[]{:S(2)}) copy-start(bf16[1,2,64,2048]{3,2,1,0:T(8,128)(2,1)} %param.29) | copy-start | bytes 1572868
  7.2 59.1 %all-gather.2.cloned.1.call-start = ((), (), s32[]{:S(2)}) async-start(), calls=%async_computation.8 | async-start | bytes 4718592 | tf_op jit(solution)/shard_map/all_gather | solution.py:468
  66.3 28.8 %collective-permute-start = (bf16[1024,2048]{1,0:T(8,128)(2,1)}, bf16[1024,2048]{1,0:T(8,128)(2,1)}, u32[]{:S(2)}, u32[]{:S(2)}) collective-permute-start(bf16[1024,2048]{1,0:T(8,128)(2,1)} %all-gather.2.cloned.1.call-done.w_ref), channel_id=1, source_target_pairs={{0,1},{1,0},{2,3},{3,2},{4,5},{5,4},{6,7},{7,6},{8,9},{9,8},{10,11... | collective-permute-start | bytes 12582920 | tf_op jit(solution)/shard_map/ppermute | solution.py:469
  68.6 17.9 %all-to-all-start = ((bf16[16,32,512]{2,1,0:T(8,128)(2,1)}), bf16[16,32,512]{2,1,0:T(8,128)(2,1)S(1)}, u32[]{:S(2)}, u32[]{:S(2)}) async-start(bf16[16,32,512]{2,1,0:T(8,128)(2,1)} %broadcast_in_dim.28), calls=%async_computation | async-start | bytes 1048576 | tf_op jit(solution)/shard_map/all_to_all | solution.py:461
  86.5 5.7 %copy-start.15 = (bf16[16,32,512]{2,1,0:T(8,128)(2,1)}, bf16[16,32,512]{2,1,0:T(8,128)(2,1)S(1)}, u32[]{:S(2)}) copy-start(bf16[16,32,512]{2,1,0:T(8,128)(2,1)S(1)} %all-to-all-done) | copy-start | bytes 1572868
  86.5 5.7 %copy-start.20 = (bf16[1,2,64,2048]{3,2,1,0:T(8,128)(2,1)S(1)}, bf16[1,2,64,2048]{3,2,1,0:T(8,128)(2,1)}, u32[]{:S(2)}) copy-start(bf16[1,2,64,2048]{3,2,1,0:T(8,128)(2,1)} %param.15) | copy-start | bytes 1572868
  86.5 5.7 %copy-start.24 = (bf16[1,2,64,256]{3,2,1,0:T(8,128)(2,1)S(1)}, bf16[1,2,64,256]{3,2,1,0:T(8,128)(2,1)}, u32[]{:S(2)}) copy-start(bf16[1,2,64,256]{3,2,1,0:T(8,128)(2,1)} %param.16) | copy-start | bytes 196612
  86.5 5.7 %copy-start.25 = (bf16[1,2,64,256]{3,2,1,0:T(8,128)(2,1)S(1)}, bf16[1,2,64,256]{3,2,1,0:T(8,128)(2,1)}, u32[]{:S(2)}) copy-start(bf16[1,2,64,256]{3,2,1,0:T(8,128)(2,1)} %param.17) | copy-start | bytes 196612
  86.5 49.9 %all-to-all-start.2 = ((bf16[128,8,1664]{2,1,0:T(8,128)(2,1)}), bf16[128,8,1664]{2,1,0:T(8,128)(2,1)}, u32[]{:S(2)}, u32[]{:S(2)}) async-start(bf16[128,8,1664]{2,1,0:T(8,128)(2,1)} %bitcast.15), calls=%async_computation.2 | async-start | bytes 6815744 | tf_op jit(solution)/shard_map/all_to_all | solution.py:436
  92.3 2.9 copy-start.4
  92.3 2.9 copy-start.9
  92.3 2.9 copy-start.18
  136.4 46.8 %all-to-all-start.1 = ((bf16[128,8,1536]{2,1,0:T(8,128)(2,1)}), bf16[128,8,1536]{2,1,0:T(8,128)(2,1)S(1)}, u32[]{:S(2)}, u32[]{:S(2)}) async-start(bf16[128,8,1536]{2,1,0:T(8,128)(2,1)} %bitcast.11), calls=%async_computation.1 | async-start | bytes 6291456 | tf_op jit(solution)/shard_map/all_to_all | solution.py:436
  270.6 46.8 %all-to-all-start.3 = ((bf16[128,8,1536]{2,1,0:T(8,128)(2,1)}), bf16[128,8,1536]{2,1,0:T(8,128)(2,1)S(1)}, u32[]{:S(2)}, u32[]{:S(2)}) async-start(bf16[128,8,1536]{2,1,0:T(8,128)(2,1)} %bitcast.64), calls=%async_computation.3 | async-start | bytes 6291456 | tf_op jit(solution)/shard_map/all_to_all | solution.py:436
  317.4 16.9 %copy-start.2 = (bf16[128,8,1536]{2,1,0:T(8,128)(2,1)}, bf16[128,8,1536]{2,1,0:T(8,128)(2,1)S(1)}, u32[]{:S(2)}) copy-start(bf16[128,8,1536]{2,1,0:T(8,128)(2,1)S(1)} %all-to-all-done.3) | copy-start | bytes 9437188
  317.4 24.7 %all-to-all-start.6 = ((bf16[128,16,256]{2,1,0:T(8,128)(2,1)}), bf16[128,16,256]{2,1,0:T(8,128)(2,1)}, u32[]{:S(2)}, u32[]{:S(2)}) async-start(bf16[128,16,256]{2,1,0:T(8,128)(2,1)} %bitcast.46), calls=%async_computation.6 | async-start | bytes 2097152 | tf_op jit(solution)/shard_map/all_to_all | solution.py:599
  342.1 23.4 %copy-start.26 = (bf16[768,2048]{1,0:T(8,128)(2,1)S(1)}, bf16[768,2048]{1,0:T(8,128)(2,1)}, u32[]{:S(2)}) copy-start(bf16[768,2048]{1,0:T(8,128)(2,1)} %get-tuple-element.50.xc_ref) | copy-start | bytes 9437188
  342.1 16.8 %all-to-all-start.5 = ((bf16[16,32,512]{2,1,0:T(8,128)(2,1)}), bf16[16,32,512]{2,1,0:T(8,128)(2,1)}, u32[]{:S(2)}, u32[]{:S(2)}) async-start(bf16[16,32,512]{2,1,0:T(8,128)(2,1)} %bitcast.51), calls=%async_computation.5 | async-start | bytes 1048576 | tf_op jit(solution)/shard_map/all_to_all | solution.py:594
  360.0 26.5 %all-to-all-start.7 = ((bf16[128,16,256]{2,1,0:T(8,128)(2,1)}), bf16[128,16,256]{2,1,0:T(8,128)(2,1)}, u32[]{:S(2)}, u32[]{:S(2)}) async-start(bf16[128,16,256]{2,1,0:T(8,128)(2,1)} %broadcast_in_dim.31), calls=%async_computation.7 | async-start | bytes 2097152 | tf_op jit(solution)/shard_map/all_to_all | solution.py:603
  371.3 11.3 %copy-start.3 = (bf16[128,8,1536]{2,1,0:T(8,128)(2,1)S(1)}, bf16[128,8,1536]{2,1,0:T(8,128)(2,1)}, u32[]{:S(2)}) copy-start(bf16[128,8,1536]{2,1,0:T(8,128)(2,1)} %copy-done.2) | copy-start | bytes 9437188
  371.3 11.3 %copy-start.7 = (f32[128,2048]{1,0:T(8,128)S(1)}, f32[128,2048]{1,0:T(8,128)}, u32[]{:S(2)}) copy-start(f32[128,2048]{1,0:T(8,128)} %copy-done.5) | copy-start | bytes 3145732
  382.6 7.9 %copy-start.1 = (bf16[256,2048]{1,0:T(8,128)(2,1)S(1)}, bf16[256,2048]{1,0:T(8,128)(2,1)}, u32[]{:S(2)}) copy-start(bf16[256,2048]{1,0:T(8,128)(2,1)} %param.21) | copy-start | bytes 3145732
  (19 other events, 23.3 us)
Sparse Core Ops, SparseCore 0:
  10.3 56.0 all-gather.1
